TPU v7x, 256 devices: a whole 4x4x8 slice. The times are simulated.
256 devices in a mesh: outer: 8 (over z), inner: 32 (over x, y, core).
Axes of the slice: x: 4, y: 4, z: 8, core: 2. Of those that a mesh axis runs over, the one named last changes fastest.
Arguments:
- b_leaf: float32 [65536, 64], P(('outer', 'inner')), may hold values from -6 to 6
- b_sep: float32 [2048, 64], P(('outer', 'inner')), may hold values from -6 to 6
- b_root: float32 [2048, 64], P(('outer', 'inner')), may hold values from -6 to 6
- leaf_linv: float32 [65536, 256], P(('outer', 'inner')), as said below
- leaf_uinv: float32 [65536, 256], P(('outer', 'inner')), as said below
- leaf_lower: float32 [65536, 256], P(('outer', 'inner')), as said below
- leaf_upper: float32 [65536, 256], P(('outer', 'inner')), as said below
- sep_rows: int32 [256, 256], P(('outer', 'inner')), may hold values from 0 to 255, as said below
- sep_linv: float32 [2048, 256], P(('outer', 'inner')), as said below
- sep_uinv: float32 [2048, 256], P(('outer', 'inner')), as said below
- sep_lower: float32 [2048, 2048], P(None, ('outer', 'inner')), as said below
- sep_upper: float32 [2048, 2048], P(('outer', 'inner')), as said below
- root_linv: float32 [2048, 2048], P(('outer', 'inner')), as said below
- root_uinv: float32 [2048, 2048], P(('outer', 'inner')), as said below
- basis_leaf: float32 [65536, 512], P(('outer', 'inner')), as said below
- basis_sep: float32 [2048, 512], P(('outer', 'inner')), as said below
- basis_root: float32 [2048, 512], P(('outer', 'inner')), as said below
- g_blocks: float32 [262144, 128], P(('outer', 'inner')), may hold values from -0.25 to 0.25
- c_blocks: float32 [262144, 128], P(('outer', 'inner')), may hold values from -0.25 to 0.25
- block_cols: int32 [512, 4], P(('outer', 'inner')), may hold values from 0 to 1
Outputs:
- v_leaf: float32 [65536, 64], P(('outer', 'inner'))
- v_sep: float32 [2048, 64], P(('outer', 'inner'))
- v_root: float32 [2048, 64], P(('outer', 'inner'))
- coefficients: float32 [512, 64], replicated
- reduced_g: float32 [64, 64], replicated
- reduced_c: float32 [64, 64], replicated
Inputs may be any that keep to these rules, and one draw needn't show every extreme that they name: `sep_rows`: each row holds 256 distinct numbers; every row names 0 and 255. `leaf_linv`: lower triangular in each diagonal block of the stack, nonzero diagonal. `leaf_uinv`: upper triangular in each diagonal block of the stack, nonzero diagonal. `sep_linv`: lower triangular in each block of 256 rows, nonzero diagonal. `sep_uinv`: upper triangular in each block of 256 rows, nonzero diagonal. `root_linv`: lower triangular, nonzero diagonal. `root_uinv`: upper triangular, nonzero diagonal. `leaf_lower`: entries of order one over the square root of 256. `leaf_upper`: entries of order one over the square root of 256. `sep_lower`: entries of order one over the square root of the number of its columns. `sep_upper`: entries of order one over the square root of 2048. basis_leaf, basis_sep and basis_root stacked by rows form Q with Q^T Q = 69632 I up to float32 rounding. `basis_sep`: part of the stacked Q described with basis_leaf. `basis_root`: part of the stacked Q described with basis_leaf.
All inputs are finite; a program needn't handle non-finite values.
Results may differ from a plain program's by a relative error of at most 0.0003.
Values sent between devices are 32-bit elements; how exact they have to be, the bound alone decides.
A program may use at most 64 MiB of HBM per device.

v0:
```python
import jax
import jax.numpy as jnp
from jax import lax
from jax.sharding import PartitionSpec as P


def matmul_exact(left, right):
    return jnp.dot(left, right, precision=lax.Precision.HIGHEST, preferred_element_type=jnp.float32)


def contract_rows(left, right):
    return lax.dot_general(
        left,
        right,
        (((0,), (0,)), ((), ())),
        precision=lax.Precision.HIGHEST,
        preferred_element_type=jnp.float32,
    )


def shards(
    b_leaf,
    b_sep,
    b_root,
    leaf_linv,
    leaf_uinv,
    leaf_lower,
    leaf_upper,
    sep_rows,
    sep_linv,
    sep_uinv,
    sep_lower,
    sep_upper,
    root_linv,
    root_uinv,
    basis_leaf,
    basis_sep,
    basis_root,
    g_blocks,
    c_blocks,
    block_cols,
):
    ports = b_leaf.shape[1]
    sep_local = b_sep.shape[0]
    root_local = b_root.shape[0]
    sep_width = sep_linv.shape[1]
    selector = (sep_rows[0][:, None] == jnp.arange(sep_width, dtype=jnp.int32)[None, :]).astype(
        jnp.float32
    )
    y_leaf = matmul_exact(leaf_linv, b_leaf)
    contrib = matmul_exact(leaf_lower, y_leaf)
    t_sep = lax.psum_scatter(
        contract_rows(selector, contrib), "inner", scatter_dimension=0, tiled=True
    )
    sep_whole = lax.all_gather(b_sep - t_sep, "inner", axis=0, tiled=True)
    y_sep = matmul_exact(sep_linv, sep_whole)
    t_root = lax.psum_scatter(
        matmul_exact(sep_lower, y_sep), ("outer", "inner"), scatter_dimension=0, tiled=True
    )
    root_rhs = lax.all_gather(b_root - t_root, ("outer", "inner"), axis=0, tiled=True)
    y_root = matmul_exact(root_linv, root_rhs)
    y_root_all = lax.all_gather(y_root, ("outer", "inner"), axis=0, tiled=True)
    x_root = matmul_exact(root_uinv, y_root_all)
    x_root_all = lax.all_gather(x_root, ("outer", "inner"), axis=0, tiled=True)
    z_sep = y_sep - matmul_exact(sep_upper, x_root_all)
    z_sep_all = lax.all_gather(z_sep, "inner", axis=0, tiled=True)
    x_sep = matmul_exact(sep_uinv, z_sep_all)
    x_sep_all = lax.all_gather(x_sep, "inner", axis=0, tiled=True)
    coupled = matmul_exact(selector, x_sep_all)
    x_leaf = matmul_exact(leaf_uinv, y_leaf - matmul_exact(leaf_upper, coupled))
    node_count = float(
        lax.axis_size("outer") * lax.axis_size("inner") * (b_leaf.shape[0] + sep_local + root_local)
    )
    pieces_x = (x_leaf, x_sep, x_root)
    pieces_q = (basis_leaf, basis_sep, basis_root)
    projected = (
        contract_rows(basis_leaf, x_leaf)
        + contract_rows(basis_sep, x_sep)
        + contract_rows(basis_root, x_root)
    )
    coefficients = lax.psum(projected, ("outer", "inner")) / node_count
    cleaned = [
        values - matmul_exact(basis, coefficients) for basis, values in zip(pieces_q, pieces_x)
    ]
    local_gram = (
        contract_rows(cleaned[0], cleaned[0])
        + contract_rows(cleaned[1], cleaned[1])
        + contract_rows(cleaned[2], cleaned[2])
    )
    gram_matrix = lax.psum(local_gram, ("outer", "inner")) / node_count
    chol_lower = jnp.linalg.cholesky(gram_matrix)
    inverse_lower = lax.linalg.triangular_solve(
        chol_lower, jnp.eye(ports, dtype=jnp.float32), left_side=True, lower=True
    )
    v_leaf = matmul_exact(cleaned[0], inverse_lower.T)
    v_sep = matmul_exact(cleaned[1], inverse_lower.T)
    v_root = matmul_exact(cleaned[2], inverse_lower.T)
    block_rows = block_cols.shape[0]
    stored = block_cols.shape[1]
    block_size = g_blocks.shape[1]
    blocked = v_leaf.reshape(block_rows, block_size, ports)
    picked = blocked[block_cols]
    g_tiles = g_blocks.reshape(block_rows, stored, block_size, block_size)
    c_tiles = c_blocks.reshape(block_rows, stored, block_size, block_size)
    g_image = jnp.einsum("rwij,rwjp->rip", g_tiles, picked, precision=lax.Precision.HIGHEST)
    c_image = jnp.einsum("rwij,rwjp->rip", c_tiles, picked, precision=lax.Precision.HIGHEST)
    g_local = jnp.einsum("rip,riq->pq", blocked, g_image, precision=lax.Precision.HIGHEST)
    c_local = jnp.einsum("rip,riq->pq", blocked, c_image, precision=lax.Precision.HIGHEST)
    g_summed, c_summed = lax.psum((g_local, c_local), ("outer", "inner"))
    return (v_leaf, v_sep, v_root, coefficients, g_summed / node_count, c_summed / node_count)


def solution(mesh):
    return jax.shard_map(
        shards,
        mesh=mesh,
        in_specs=(
            P(("outer", "inner"), None),
            P(("outer", "inner"), None),
            P(("outer", "inner"), None),
            P(("outer", "inner"), None),
            P(("outer", "inner"), None),
            P(("outer", "inner"), None),
            P(("outer", "inner"), None),
            P(("outer", "inner"), None),
            P(("outer", "inner"), None),
            P(("outer", "inner"), None),
            P(None, ("outer", "inner")),
            P(("outer", "inner"), None),
            P(("outer", "inner"), None),
            P(("outer", "inner"), None),
            P(("outer", "inner"), None),
            P(("outer", "inner"), None),
            P(("outer", "inner"), None),
            P(("outer", "inner"), None),
            P(("outer", "inner"), None),
            P(("outer", "inner"), None),
        ),
        out_specs=(
            P(("outer", "inner"), None),
            P(("outer", "inner"), None),
            P(("outer", "inner"), None),
            P(),
            P(),
            P(),
        ),
        check_vma=False,
    )
```

profile of v0, /device:TPU:1, one launch (start us, length us, event | category | flops | bytes accessed | tf_op | source)
XLA Modules:
  0.0 1057.3 jit_solution(8577901284034292284)
XLA Ops:
  7.2 0.0 all-reduce.9.cloned.1.call-start
  7.2 1.4 fusion.16
  8.6 0.4 fusion.17
  9.0 0.7 copy-done.16
  9.7 1.0 fusion.8
  10.8 0.0 all-reduce.9.cloned.1.call-update
  10.8 0.0 all-reduce.11.cloned.1.call-start
  10.8 0.7 copy-done.20
  11.5 0.6 dynamic-slice
  12.7 112.8 %all-reduce.9.cloned.1.call-done = f32[256,64]{1,0:T(8,128)} async-done(((f32[256,64]{1,0:T(8,128)}), f32[256,64]{1,0:T(8,128)}) %all-reduce.9.cloned.1.call-update) | async-done | bytes 65552
  125.5 0.7 dynamic-slice_subtract_fusion.1
  126.2 25.7 %all_gather.18 = f32[256,64]{1,0:T(8,128)S(1)} all-gather(f32[8,64]{1,0:T(8,128)S(1)} %dynamic-slice_subtract_fusion.1), channel_id=1, replica_groups=mesh['outer'=8,'inner'=32] {'inner'}, dimensions={0}, use_global_device_ids=true | all-gather | bytes 67584 | tf_op jit(solution)/shard_map/all_gather | solution.py:55
  151.8 0.2 fusion.18
  152.0 0.7 copy-done.8
  152.7 0.6 convolution_bitcast_fusion
  153.3 1.3 copy.47
  154.7 0.0 all-reduce.7.cloned.1.call-start
  154.8 0.6 copy-done.19
  155.4 0.1 reshape.36
  155.4 251.8 %all-reduce.11.cloned.1.call-done = f32[2048,64]{1,0:T(8,128)} async-done(((f32[2048,64]{1,0:T(8,128)}), f32[2048,64]{1,0:T(8,128)}) %all-reduce.11.cloned.1.call-update) | async-done | bytes 524304
  407.2 0.7 dynamic-slice_subtract_fusion
  407.9 63.2 %all_gather.19 = f32[2048,64]{1,0:T(8,128)S(1)} all-gather(f32[8,64]{1,0:T(8,128)S(1)} %dynamic-slice_subtract_fusion), channel_id=1, replica_groups=mesh['outer'=8,'inner'=32] {'outer','inner'}, dimensions={0}, use_global_device_ids=true | all-gather | bytes 526336 | tf_op jit(solution)/shard_map/all_gather | solution.py:60
  471.1 0.7 convolution_bitcast_fusion.8
  471.7 60.2 %all_gather.20 = f32[2048,64]{1,0:T(8,128)S(1)} all-gather(f32[8,64]{1,0:T(8,128)S(1)} %convolution_bitcast_fusion.8), channel_id=1, replica_groups=mesh['outer'=8,'inner'=32] {'outer','inner'}, dimensions={0}, use_global_device_ids=true | all-gather | bytes 526336 | tf_op jit(solution)/shard_map/all_gather | solution.py:62
  532.0 0.7 fusion.19
  532.6 60.4 %all_gather.21 = f32[2048,64]{1,0:T(8,128)S(1)} all-gather(f32[8,64]{1,0:T(8,128)S(1)} %bitcast.121), channel_id=1, replica_groups=mesh['outer'=8,'inner'=32] {'outer','inner'}, dimensions={0}, use_global_device_ids=true | all-gather | bytes 526336 | tf_op jit(solution)/shard_map/all_gather | solution.py:64
  593.1 0.7 fusion.5
  593.7 23.3 %all_gather.22 = f32[256,64]{1,0:T(8,128)S(1)} all-gather(f32[8,64]{1,0:T(8,128)S(1)} %fusion.5), channel_id=1, replica_groups=mesh['outer'=8,'inner'=32] {'inner'}, dimensions={0}, use_global_device_ids=true | all-gather | bytes 67584 | tf_op jit(solution)/shard_map/all_gather | solution.py:66
  617.0 0.2 fusion.20
  617.2 23.0 %all_gather.23 = f32[256,64]{1,0:T(8,128)S(1)} all-gather(f32[8,64]{1,0:T(8,128)S(1)} %bitcast.122), channel_id=1, replica_groups=mesh['outer'=8,'inner'=32] {'inner'}, dimensions={0}, use_global_device_ids=true | all-gather | bytes 67584 | tf_op jit(solution)/shard_map/all_gather | solution.py:68
  640.2 0.3 fusion.6
  640.6 0.3 fusion.22
  640.9 0.0 copy-done.13
  640.9 0.3 fusion.23
  641.3 0.4 fusion.2
  641.6 0.4 fusion.21
  642.0 1.1 fusion.1
  643.1 237.7 %all-reduce.7.cloned.1.call-done = f32[512,64]{0,1:T(8,128)} async-done(((f32[512,64]{0,1:T(8,128)}), f32[512,64]{0,1:T(8,128)}) %all-reduce.7.cloned.1.call-update) | async-done | bytes 131088 | tf_op jit(solution)/shard_map/psum | solution.py:81
  880.8 0.9 broadcast_multiply_fusion
  881.8 0.6 convolution_subtract_fusion
  882.4 0.2 fusion.4
  882.6 0.2 fusion.3
  882.8 0.2 fusion.24
  883.0 0.2 convolution_add_fusion.2
  883.3 0.2 convolution_add_fusion.1
  883.5 76.0 %psum.29 = f32[64,64]{0,1:T(8,128)S(1)} all-reduce(f32[64,64]{0,1:T(8,128)S(1)} %convolution_add_fusion.1), channel_id=1, replica_groups=mesh['outer'=8,'inner'=32] {'outer','inner'}, use_global_device_ids=true, to_apply=%region_3.0 | all-reduce | flops 4096 | bytes 32768 | tf_op jit(solution)/shard_map/psum | solution.py:90
  959.6 0.1 copy.51
  959.7 5.8 cholesky.17
  965.6 0.6 compare_reduce_fusion
  966.2 0.7 fusion.12
  966.9 4.9 custom-call.6
  971.8 0.2 fusion.13
  972.0 0.2 fusion.25
  972.2 0.8 fusion.27
  973.0 0.8 fusion.26
  973.7 0.6 gather_fusion
  974.3 0.7 convolution_bitcast_fusion.1
  975.0 0.2 convolution_bitcast_fusion.4
  975.2 0.2 copy-done.4
  975.4 0.7 convolution_bitcast_fusion.2
  976.0 0.2 convolution_bitcast_fusion.5
  976.2 73.1 %all-reduce.2 = (f32[64,64]{0,1:T(8,128)S(1)}, f32[64,64]{0,1:T(8,128)S(1)}) all-reduce(f32[64,64]{0,1:T(8,128)S(1)} %convolution_bitcast_fusion.5, f32[64,64]{0,1:T(8,128)S(1)} %convolution_bitcast_fusion.4), channel_id=1, replica_groups=mesh['outer'=8,'inner'=32] {'outer','inner'}, use_global_device_ids=true, to_apply=%region_6.7 | all-reduce | flops 8192 | bytes 65536 | tf_op jit(solution)/shard_map/psum | solution.py:109
  1049.4 0.7 copy.57
  1050.1 0.7 copy.58
  (45 shorter events, 0.2 us)
Async XLA Ops:
  7.2 967.2 %copy-start = (f32[1024,128]{1,0:T(8,128)S(1)}, f32[1024,128]{1,0:T(8,128)}, u32[]{:S(2)}) copy-start(f32[1024,128]{1,0:T(8,128)} %param.38) | copy-start | bytes 1572868
  7.2 1.5 copy-start.6
  7.2 118.3 %all-reduce.9.cloned.1.call-start = ((), (), s32[]{:S(2)}) async-start(), calls=%async_computation.1 | async-start | bytes 262144
  9.0 0.7 copy-start.16
  10.8 396.5 %all-reduce.11.cloned.1.call-start = ((), (), s32[]{:S(2)}) async-start(), calls=%async_computation.2 | async-start | bytes 2097152
  10.8 0.7 copy-start.20
  11.5 114.0 %copy-start.17 = (f32[8,64]{1,0:T(8,128)S(1)}, f32[8,64]{1,0:T(8,128)}, u32[]{:S(2)}) copy-start(f32[8,64]{1,0:T(8,128)} %param.21) | copy-start | bytes 6148
  126.2 25.7 %copy-start.14 = (f32[8,256]{1,0:T(8,128)S(1)}, f32[8,256]{1,0:T(8,128)}, u32[]{:S(2)}) copy-start(f32[8,256]{1,0:T(8,128)} %param.28) | copy-start | bytes 24580
  151.8 0.8 copy-start.8
  154.7 0.7 copy-start.19
  154.7 252.5 %copy-start.18 = (f32[8,64]{1,0:T(8,128)S(1)}, f32[8,64]{1,0:T(8,128)}, u32[]{:S(2)}) copy-start(f32[8,64]{1,0:T(8,128)} %param.22) | copy-start | bytes 6148
  154.7 726.1 %all-reduce.7.cloned.1.call-start = ((), (), s32[]{:S(2)}) async-start(), calls=%async_computation | async-start | bytes 262144 | tf_op jit(solution)/shard_map/psum | solution.py:81
  407.9 63.2 %copy-start.9 = (f32[8,2048]{1,0:T(8,128)S(1)}, f32[8,2048]{1,0:T(8,128)}, u32[]{:S(2)}) copy-start(f32[8,2048]{1,0:T(8,128)} %param.32) | copy-start | bytes 196612
  471.7 60.2 %copy-start.10 = (f32[8,2048]{1,0:T(8,128)S(1)}, f32[8,2048]{1,0:T(8,128)}, u32[]{:S(2)}) copy-start(f32[8,2048]{1,0:T(8,128)} %param.33) | copy-start | bytes 196612
  532.6 60.4 %copy-start.11 = (f32[8,2048]{1,0:T(8,128)S(1)}, f32[8,2048]{1,0:T(8,128)}, u32[]{:S(2)}) copy-start(f32[8,2048]{1,0:T(8,128)} %param.31) | copy-start | bytes 196612
  593.7 23.3 %copy-start.15 = (f32[8,256]{1,0:T(8,128)S(1)}, f32[8,256]{1,0:T(8,128)}, u32[]{:S(2)}) copy-start(f32[8,256]{1,0:T(8,128)} %param.29) | copy-start | bytes 24580
  617.2 23.4 %copy-start.12 = (f32[8,512]{1,0:T(8,128)S(1)}, f32[8,512]{1,0:T(8,128)}, u32[]{:S(2)}) copy-start(f32[8,512]{1,0:T(8,128)} %param.35) | copy-start | bytes 49156
  640.2 0.7 copy-start.13
  640.2 1.0 copy-start.5
  640.6 1.1 copy-start.7
  640.9 1.1 copy-start.1
  881.8 0.8 copy-start.2
  972.2 3.8 copy-start.3
  974.3 1.0 copy-start.4
Sparse Core Ops, SparseCore 0:
  11.8 113.6 all-reduce.8
  154.8 252.3 all-reduce.10
  643.3 237.5 all-reduce.6
where the time goes:
time: 1060 us
  waiting for transfers between devices  602 us (57%)
  blocking collectives  405 us (38%)
  between operations  14.7 us (1%)
  other arithmetic  14.4 us (1%)
  matrix products  14 us (1%)
    unnamed x5, waiting for transfers between devices  365 us
    psum x1, waiting for transfers between devices, shards(): coefficients = lax.psum(projected, ('outer', 'inner')) / node_count  238 us
    psum x1, blocking collectives, shards(): gram_matrix = lax.psum(local_gram, ('outer', 'inner')) / node_count  76 us
    psum x1, blocking collectives, shards(): g_summed, c_summed = lax.psum((g_local, c_local), ('outer', 'inner'))  73.1 us
    all_gather x1, blocking collectives, shards(): lax.all_gather(b_root - t_root, ('outer', 'inner'), axis=0, tiled=True)  63.2 us
    all_gather x1, blocking collectives, shards(): x_root_all = lax.all_gather(x_root, ('outer', 'inner'), axis=0, tiled=True)  60.4 us
    all_gather x1, blocking collectives, shards(): y_root_all = lax.all_gather(y_root, ('outer', 'inner'), axis=0, tiled=True)  60.2 us
    all_gather x1, blocking collectives, shards(): sep_whole = lax.all_gather(b_sep - t_sep, 'inner', axis=0, tiled=True)  25.7 us
  transfers between devices with their start and end apart: 3, of which 3 were waited for; matrix products, arithmetic and copies ran while one was open for 0% of the time, Pallas kernels for 0%

commit v1 on v0

--- a/solution.py
+++ b/solution.py
@@ -2,6 +2,7 @@
 import jax.numpy as jnp
 from jax import lax
 from jax.sharding import PartitionSpec as P
+from jax.lax import all_gather
 
 
 def matmul_exact(left, right):
@@ -87,7 +88,8 @@
         + contract_rows(cleaned[1], cleaned[1])
         + contract_rows(cleaned[2], cleaned[2])
     )
-    gram_matrix = lax.psum(local_gram, ("outer", "inner")) / node_count
+    step_on_the_tiles = lambda target: all_gather(target, axis_name=("outer", "inner")).sum(axis=0)
+    gram_matrix = step_on_the_tiles(local_gram) / node_count
     chol_lower = jnp.linalg.cholesky(gram_matrix)
     inverse_lower = lax.linalg.triangular_solve(
         chol_lower, jnp.eye(ports, dtype=jnp.float32), left_side=True, lower=True

time: 1060 us -> 1110 us (1.047)
  waiting for transfers between devices: 602 us -> 719 us
  blocking collectives: 405 us -> 330 us
    all_gather x0 -> x1, waiting for transfers between devices: none -> 117 us  [shards(): all_gather(target, axis_name=('outer', 'inner')).sum(axis=0)]
    psum x1 -> x0, blocking collectives: 76 us -> none  [shards(): gram_matrix = lax.psum(local_gram, ('outer', 'inner')) / node_count]
    unnamed x5 -> x6, waiting for transfers between devices: 365 us -> 364 us
  transfers between devices with their start and end apart: 3 -> 4, of which waited for: 3 -> 4; matrix products, arithmetic and copies ran while one was open for 0% -> 0% of each run, Pallas kernels for 0% -> 0%
where the time goes in v1:
time: 1110 us
  waiting for transfers between devices  719 us (65%)
  blocking collectives  330 us (30%)
  matrix products  19.5 us (2%)
  other arithmetic  18.5 us (2%)
  between operations  14.7 us (1%)
    unnamed x6, waiting for transfers between devices  364 us
    psum x1, waiting for transfers between devices, shards(): coefficients = lax.psum(projected, ('outer', 'inner')) / node_count  237 us
    all_gather x1, waiting for transfers between devices, shards(): all_gather(target, axis_name=('outer', 'inner')).sum(axis=0)  117 us
    psum x1, blocking collectives, shards(): g_summed, c_summed = lax.psum((g_local, c_local), ('outer', 'inner'))  74.7 us
    all_gather x1, blocking collectives, shards(): lax.all_gather(b_root - t_root, ('outer', 'inner'), axis=0, tiled=True)  63 us
    all_gather x1, blocking collectives, shards(): x_root_all = lax.all_gather(x_root, ('outer', 'inner'), axis=0, tiled=True)  60.4 us
    all_gather x1, blocking collectives, shards(): y_root_all = lax.all_gather(y_root, ('outer', 'inner'), axis=0, tiled=True)  60.2 us
    all_gather x1, blocking collectives, shards(): sep_whole = lax.all_gather(b_sep - t_sep, 'inner', axis=0, tiled=True)  25.5 us
  transfers between devices with their start and end apart: 4, of which 4 were waited for; matrix products, arithmetic and copies ran while one was open for 0% of the time, Pallas kernels for 0%

profile of v1, /device:TPU:1, one launch (start us, length us, event | category | flops | bytes accessed | tf_op | source)
XLA Modules:
  0.0 1106.8 jit_solution(9437879770183905573)
XLA Ops:
  7.3 0.0 all-reduce.9.cloned.1.call-start
  7.3 1.5 fusion.16
  8.8 1.3 fusion.17
  10.1 1.7 fusion.8
  11.8 0.0 all-reduce.9.cloned.1.call-update
  11.9 0.0 all-reduce.11.cloned.1.call-start
  11.9 1.3 dynamic-slice
  13.8 111.8 %all-reduce.9.cloned.1.call-done = f32[256,64]{1,0:T(8,128)} async-done(((f32[256,64]{1,0:T(8,128)}), f32[256,64]{1,0:T(8,128)}) %all-reduce.9.cloned.1.call-update) | async-done | bytes 65552
  125.7 0.7 dynamic-slice_subtract_fusion.1
  126.4 25.5 %all_gather.24 = f32[256,64]{1,0:T(8,128)S(1)} all-gather(f32[8,64]{1,0:T(8,128)S(1)} %dynamic-slice_subtract_fusion.1), channel_id=1, replica_groups=mesh['outer'=8,'inner'=32] {'inner'}, dimensions={0}, use_global_device_ids=true | all-gather | bytes 67584 | tf_op jit(solution)/shard_map/all_gather | solution.py:56
  151.9 0.9 fusion.18
  152.8 1.5 convolution_bitcast_fusion
  154.2 1.4 copy.41
  155.6 0.0 all-reduce.11.cloned.1.call-update
  155.6 0.0 all-reduce.7.cloned.1.call-start
  155.7 252.5 %all-reduce.11.cloned.1.call-done = f32[2048,64]{1,0:T(8,128)} async-done(((f32[2048,64]{1,0:T(8,128)}), f32[2048,64]{1,0:T(8,128)}) %all-reduce.11.cloned.1.call-update) | async-done | bytes 524304
  408.2 0.7 dynamic-slice_subtract_fusion
  408.9 63.0 %all_gather.25 = f32[2048,64]{1,0:T(8,128)S(1)} all-gather(f32[8,64]{1,0:T(8,128)S(1)} %dynamic-slice_subtract_fusion), channel_id=1, replica_groups=mesh['outer'=8,'inner'=32] {'outer','inner'}, dimensions={0}, use_global_device_ids=true | all-gather | bytes 526336 | tf_op jit(solution)/shard_map/all_gather | solution.py:61
  471.9 1.5 convolution_bitcast_fusion.8
  473.4 60.2 %all_gather.26 = f32[2048,64]{1,0:T(8,128)S(1)} all-gather(f32[8,64]{1,0:T(8,128)S(1)} %convolution_bitcast_fusion.8), channel_id=1, replica_groups=mesh['outer'=8,'inner'=32] {'outer','inner'}, dimensions={0}, use_global_device_ids=true | all-gather | bytes 526336 | tf_op jit(solution)/shard_map/all_gather | solution.py:63
  533.7 1.5 fusion.19
  535.2 60.4 %all_gather.27 = f32[2048,64]{1,0:T(8,128)S(1)} all-gather(f32[8,64]{1,0:T(8,128)S(1)} %bitcast.123), channel_id=1, replica_groups=mesh['outer'=8,'inner'=32] {'outer','inner'}, dimensions={0}, use_global_device_ids=true | all-gather | bytes 526336 | tf_op jit(solution)/shard_map/all_gather | solution.py:65
  595.6 0.7 fusion.5
  596.2 23.2 %all_gather.28 = f32[256,64]{1,0:T(8,128)S(1)} all-gather(f32[8,64]{1,0:T(8,128)S(1)} %fusion.5), channel_id=1, replica_groups=mesh['outer'=8,'inner'=32] {'inner'}, dimensions={0}, use_global_device_ids=true | all-gather | bytes 67584 | tf_op jit(solution)/shard_map/all_gather | solution.py:67
  619.5 0.2 fusion.20
  619.6 23.0 %all_gather.29 = f32[256,64]{1,0:T(8,128)S(1)} all-gather(f32[8,64]{1,0:T(8,128)S(1)} %bitcast.124), channel_id=1, replica_groups=mesh['outer'=8,'inner'=32] {'inner'}, dimensions={0}, use_global_device_ids=true | all-gather | bytes 67584 | tf_op jit(solution)/shard_map/all_gather | solution.py:69
  642.7 0.3 fusion.6
  643.1 0.3 fusion.22
  643.4 0.3 fusion.23
  643.7 0.4 fusion.2
  644.1 0.4 fusion.21
  644.5 1.1 fusion.1
  645.6 0.0 all-reduce.7.cloned.1.call-update
  645.6 0.0 all-gather.3.cloned.1.call-start
  645.6 237.4 %all-reduce.7.cloned.1.call-done = f32[512,64]{0,1:T(8,128)} async-done(((f32[512,64]{0,1:T(8,128)}), f32[512,64]{0,1:T(8,128)}) %all-reduce.7.cloned.1.call-update) | async-done | bytes 131088 | tf_op jit(solution)/shard_map/psum | solution.py:82
  883.1 0.9 broadcast_multiply_fusion
  884.0 0.6 convolution_subtract_fusion
  884.6 0.2 fusion.4
  884.8 0.2 fusion.3
  885.0 0.2 fusion.24
  885.3 0.2 convolution_add_fusion.2
  885.5 0.9 convolution_add_fusion.1
  886.4 0.0 all-gather.3.cloned.1.call-update
  886.4 0.1 reshape.36
  886.5 117.0 %all-gather.3.cloned.1.call-done = f32[16384,64]{1,0:T(8,128)} async-done(((f32[64,64]{1,0:T(8,128)}), f32[16384,64]{1,0:T(8,128)}) %all-gather.3.cloned.1.call-update) | async-done | bytes 4194320 | tf_op jit(solution)/shard_map/all_gather | solution.py:91
  1003.6 4.0 reduce_sum.9
  1007.6 0.1 copy.42
  1007.7 0.1 copy.43
  1007.8 5.8 cholesky.17
  1013.6 0.6 compare_reduce_fusion
  1014.3 0.7 fusion.12
  1014.9 4.9 custom-call.6
  1019.8 0.2 fusion.13
  1020.1 0.2 fusion.25
  1020.3 0.8 fusion.27
  1021.1 0.8 fusion.26
  1021.8 0.6 gather_fusion
  1022.4 0.7 convolution_bitcast_fusion.1
  1023.1 0.2 convolution_bitcast_fusion.4
  1023.3 0.7 convolution_bitcast_fusion.2
  1024.0 0.2 convolution_bitcast_fusion.5
  1024.2 74.7 %all-reduce.2 = (f32[64,64]{0,1:T(8,128)S(1)}, f32[64,64]{0,1:T(8,128)S(1)}) all-reduce(f32[64,64]{0,1:T(8,128)S(1)} %convolution_bitcast_fusion.5, f32[64,64]{0,1:T(8,128)S(1)} %convolution_bitcast_fusion.4), channel_id=1, replica_groups=mesh['outer'=8,'inner'=32] {'outer','inner'}, use_global_device_ids=true, to_apply=%region_6.7 | all-reduce | flops 8192 | bytes 65536 | tf_op jit(solution)/shard_map/psum | solution.py:111
  1098.9 0.7 copy.49
  1099.6 0.7 copy.50
  (33 shorter events, 0.1 us)
Async XLA Ops:
  7.2 1015.2 %copy-start = (f32[1024,128]{1,0:T(8,128)S(1)}, f32[1024,128]{1,0:T(8,128)}, u32[]{:S(2)}) copy-start(f32[1024,128]{1,0:T(8,128)} %param.38) | copy-start | bytes 1572868
  7.2 635.5 %copy-start.11 = (s32[1,256]{1,0:T(1,128)S(1)}, s32[1,256]{1,0:T(1,128)}, u32[]{:S(2)}) copy-start(s32[1,256]{1,0:T(1,128)} %param.27) | copy-start | bytes 3076
  7.2 588.4 %copy-start.7 = (f32[8,2048]{1,0:T(8,128)S(1)}, f32[8,2048]{1,0:T(8,128)}, u32[]{:S(2)}) copy-start(f32[8,2048]{1,0:T(8,128)} %param.31) | copy-start | bytes 196612
  7.2 612.3 %copy-start.10 = (f32[8,256]{1,0:T(8,128)S(1)}, f32[8,256]{1,0:T(8,128)}, u32[]{:S(2)}) copy-start(f32[8,256]{1,0:T(8,128)} %param.29) | copy-start | bytes 24580
  7.2 635.8 %copy-start.8 = (f32[8,512]{1,0:T(8,128)S(1)}, f32[8,512]{1,0:T(8,128)}, u32[]{:S(2)}) copy-start(f32[8,512]{1,0:T(8,128)} %param.35) | copy-start | bytes 49156
  7.2 636.1 %copy-start.9 = (f32[8,512]{1,0:T(8,128)S(1)}, f32[8,512]{1,0:T(8,128)}, u32[]{:S(2)}) copy-start(f32[8,512]{1,0:T(8,128)} %param.36) | copy-start | bytes 49156
  7.2 636.5 %copy-start.5 = (f32[256,256]{1,0:T(8,128)S(1)}, f32[256,256]{1,0:T(8,128)}, u32[]{:S(2)}) copy-start(f32[256,256]{1,0:T(8,128)} %param.26) | copy-start | bytes 786436
  7.2 636.8 %copy-start.6 = (f32[256,256]{1,0:T(8,128)S(1)}, f32[256,256]{1,0:T(8,128)}, u32[]{:S(2)}) copy-start(f32[256,256]{1,0:T(8,128)} %param.24) | copy-start | bytes 786436
  7.3 637.2 %copy-start.1 = (f32[256,512]{1,0:T(8,128)S(1)}, f32[256,512]{1,0:T(8,128)}, u32[]{:S(2)}) copy-start(f32[256,512]{1,0:T(8,128)} %param.34) | copy-start | bytes 1572868
  7.3 879.1 %copy-start.12 = (s32[2,4]{1,0:T(2,128)S(1)}, s32[2,4]{1,0:T(2,128)}, u32[]{:S(2)}) copy-start(s32[2,4]{1,0:T(2,128)} %param.39) | copy-start | bytes 100
  7.3 118.4 %all-reduce.9.cloned.1.call-start = ((), (), s32[]{:S(2)}) async-start(), calls=%async_computation.2 | async-start | bytes 262144
  11.9 396.4 %all-reduce.11.cloned.1.call-start = ((), (), s32[]{:S(2)}) async-start(), calls=%async_computation.3 | async-start | bytes 2097152
  155.6 727.5 %all-reduce.7.cloned.1.call-start = ((), (), s32[]{:S(2)}) async-start(), calls=%async_computation | async-start | bytes 262144 | tf_op jit(solution)/shard_map/psum | solution.py:82
  595.6 427.7 %copy-start.4 = (f32[1024,128]{1,0:T(8,128)S(1)}, f32[1024,128]{1,0:T(8,128)}, u32[]{:S(2)}) copy-start(f32[1024,128]{1,0:T(8,128)} %param.37) | copy-start | bytes 1572868
  645.6 358.0 %all-gather.3.cloned.1.call-start = ((), (), s32[]{:S(2)}) async-start(), calls=%async_computation.1 | async-start | bytes 8421376 | tf_op jit(solution)/shard_map/all_gather | solution.py:91
  884.0 216.3 %copy-start.2 = (f32[512,64]{0,1:T(8,128)}, f32[512,64]{0,1:T(8,128)S(1)}, u32[]{:S(2)}) copy-start(f32[512,64]{0,1:T(8,128)S(1)} %broadcast_multiply_fusion) | copy-start | bytes 393220
  1020.3 80.0 %copy-start.3 = (f32[256,64]{0,1:T(8,128)}, f32[256,64]{0,1:T(8,128)S(1)}, u32[]{:S(2)}) copy-start(f32[256,64]{0,1:T(8,128)S(1)} %fusion.25) | copy-start | bytes 196612
Sparse Core Ops, SparseCore 0:
  12.0 113.6 all-reduce.8
  155.7 252.4 all-reduce.10
  645.7 237.3 all-reduce.6
  887.2 116.2 all-gather.2
